TPU v7x, 256 devices: a whole 4x4x8 slice. The times are simulated.
256 devices in a mesh: row: 64 (over z, y, x_hi), rep: 4 (over x_lo, core).
Axes of the slice: x: 4 (x_hi: 2, x_lo: 2; x = x_hi * 2 + x_lo), y: 4, z: 8, core: 2. Of those that a mesh axis runs over, the one named last changes fastest.
Arguments:
- features: float32 [65536, 256], P(('row', 'rep')), may hold values from -6 to 6
- weight: float32 [256, 256], replicated, may hold values from -0.375 to 0.375
- cotangent: float32 [65536, 256], P(('row', 'rep')), may hold values from -6 to 6
- tile_row: int32 [64, 4, 128], P('row', 'rep'), may hold values from 0 to 7
- tile_col: int32 [64, 4, 128], P('row', 'rep'), may hold values from 0 to 511, as said below
- tile_count: int32 [64, 4], P('row', 'rep'), may hold values from 2 to 128, as said below
- tile_values: float32 [64, 4, 128, 128, 128], P('row', 'rep'), may hold values from -0.09375 to 0.09375
Outputs:
- activation: float32 [65536, 256], P(('row', 'rep'))
- feature_grad: float32 [65536, 256], P(('row', 'rep'))
- weight_grad: float32 [256, 256], replicated
Inputs may be any that keep to these rules, and one draw needn't show every extreme that they name: `tile_col`: for a tile of row block b with row tile t the column tile is (b * 8 + t + o) mod 512 with -16 <= o <= 16; every device's live slots hold both o = -16 and o = 16. Slots from tile_count on are ignored, whatever they hold; some device has exactly 128 live slots.
All inputs are finite; a program needn't handle non-finite values.
Results may differ from a plain program's by a relative error of at most 0.0003.
Values sent between devices are 32-bit elements; how exact they have to be, the bound alone decides.
A program may use at most 128 MiB of HBM per device.

v0:
```python
import jax
import jax.numpy as jnp
from jax import lax
from jax.sharding import PartitionSpec as P

TILE = 128
TPB = 8
SPAN = 2


def passed_along(block, axis, distance):
    devices = range(lax.axis_size(axis))
    route = [((i - distance) % len(devices), i) for i in devices]
    return lax.ppermute(block, axis, route)


def silu_slope(pre_act):
    sigma_value = jax.nn.sigmoid(pre_act)
    return sigma_value * (1.0 + pre_act * (1.0 - sigma_value))


def band_pieces(base):
    pieces = []
    for offset in range(-SPAN, SPAN + 1):
        if offset == 0:
            pieces.append(base)
        else:
            pieces.append(passed_along(base, "row", -offset))
    return pieces


def shards(features, weight, cotangent, tile_row, tile_col, tile_count, tile_values):
    precise = lax.Precision.HIGHEST
    tile_rows = tile_row[0, 0]
    tile_cols = tile_col[0, 0]
    slot_count = tile_rows.shape[0]
    tile_vals = tile_values[0, 0]
    feat_width = features.shape[1]
    is_live = jnp.arange(slot_count, dtype=jnp.int32) < tile_count[0, 0]
    own_block = lax.all_gather(features, "rep", axis=0, tiled=True)
    window = jnp.concatenate(band_pieces(own_block), axis=0).reshape(-1, TILE, feat_width)
    window_tiles = window.shape[0]
    row_index = lax.axis_index("row")
    total_tiles = TPB * lax.axis_size("row")
    position = jnp.mod(tile_cols - (row_index - SPAN) * TPB, total_tiles)
    gathered = jnp.take(window, position, axis=0)
    products = jnp.einsum("tij,tjf->tif", tile_vals, gathered, precision=precise)
    row_hot = (
        (tile_rows[None, :] == jnp.arange(TPB, dtype=jnp.int32)[:, None]) & is_live[None, :]
    ).astype(jnp.float32)
    partial_value = jnp.einsum("bt,tif->bif", row_hot, products, precision=precise).reshape(
        -1, feat_width
    )
    own_share = lax.psum_scatter(partial_value, "rep", scatter_dimension=0, tiled=True)
    pre_act = jnp.dot(own_share, weight, precision=precise, preferred_element_type=jnp.float32)
    activation = jax.nn.silu(pre_act)
    grad_pre = cotangent * silu_slope(pre_act)
    grad_agg = jnp.dot(grad_pre, weight.T, precision=precise, preferred_element_type=jnp.float32)
    local_wgrad = jnp.dot(
        own_share.T, grad_pre, precision=precise, preferred_element_type=jnp.float32
    )
    weight_grad = lax.psum(local_wgrad, ("row", "rep"))
    grad_block = lax.all_gather(grad_agg, "rep", axis=0, tiled=True).reshape(TPB, TILE, feat_width)
    picked = jnp.take(grad_block, tile_rows, axis=0)
    backward = jnp.einsum("tij,tif->tjf", tile_vals, picked, precision=precise)
    pos_hot = (
        (position[None, :] == jnp.arange(window_tiles, dtype=jnp.int32)[:, None]) & is_live[None, :]
    ).astype(jnp.float32)
    window_grad = jnp.einsum("wt,tjf->wjf", pos_hot, backward, precision=precise)
    window_grad = window_grad.reshape(2 * SPAN + 1, -1, feat_width)
    summed = window_grad[SPAN]
    for offset in range(-SPAN, SPAN + 1):
        if offset != 0:
            summed = summed + passed_along(window_grad[SPAN + offset], "row", offset)
    feature_grad = lax.psum_scatter(summed, "rep", scatter_dimension=0, tiled=True)
    return (activation, feature_grad, weight_grad)


def solution(mesh):
    placed = (
        P(("row", "rep"), None),
        P(),
        P(("row", "rep"), None),
        P("row", "rep", None),
        P("row", "rep", None),
        P("row", "rep"),
        P("row", "rep", None, None, None),
    )
    return jax.shard_map(
        shards,
        mesh=mesh,
        in_specs=placed,
        out_specs=(P(("row", "rep"), None), P(("row", "rep"), None), P()),
        check_vma=False,
    )
```

profile of v0, /device:TPU:1, one launch (start us, length us, event | category | flops | bytes accessed | tf_op | source)
XLA Modules:
  0.0 616.9 jit_solution(15306313396574777297)
XLA Ops:
  8.0 29.3 %all-gather.3.cloned.1.call-done = f32[1024,256]{1,0:T(8,128)} async-done(((f32[256,256]{1,0:T(8,128)}), f32[1024,256]{1,0:T(8,128)}) %all-gather.3.cloned.1.call-update) | async-done | bytes 1048592 | tf_op jit(solution)/shard_map/all_gather | solution.py:40
  38.5 2.4 collective-permute-start.1
  40.9 4.0 collective-permute-start.3
  48.4 35.2 %collective-permute-done = f32[1024,256]{1,0:T(8,128)S(1)} collective-permute-done((f32[1024,256]{1,0:T(8,128)}, f32[1024,256]{1,0:T(8,128)S(1)}, u32[]{:S(2)}, u32[]{:S(2)}) %collective-permute-start) | collective-permute-done | bytes 1048608 | tf_op jit(solution)/shard_map/ppermute | solution.py:14
  84.7 6.0 collective-permute-done.1
  96.2 12.5 %gather_fusion = f32[128,128,256]{2,1,0:T(8,128)} fusion(f32[40,128,256]{2,1,0:T(8,128)} %bitcast.4, s32[1024]{0:T(1024)S(1)} %pad_clamp_fusion.1), kind=kCustom, calls=%fused_computation | custom fusion | bytes 33554944 | tf_op jit(solution)/shard_map/jit(_take)/gather | solution.py:46
  108.7 34.5 %fusion.6 = f32[128,256,128]{2,1,0:T(8,128)} fusion(f32[128,128,256]{2,1,0:T(8,128)} %gather_fusion, f32[1,1,128,128,128]{4,3,2,1,0:T(8,128)} %param.13, pred[128]{0:T(512)(128)(4,1)S(1)} %get-tuple-element.3), kind=kOutput, calls=%fused_computation.8 | convolution fusion | flops 6446645248 | bytes 41943168 | tf_op jit(solution)/shard_map/tij,tjf->tif/dot_general | solution.py:47
  143.2 17.7 %copy.16 = f32[128,256,128]{1,0,2:T(8,128)} copy(f32[128,256,128]{2,1,0:T(8,128)} %fusion.6) | data formatting | bytes 33554432 | tf_op jit(solution)/shard_map/tij,tjf->tif/dot_general | solution.py:47
  161.0 9.1 %fusion.2 = f32[8,128,256]{2,0,1:T(8,128)S(1)} fusion(f32[128,256,128]{1,0,2:T(8,128)} %copy.16, s32[128]{0:T(128)S(1)} %bitcast.55, pred[128]{0:T(512)(128)(4,1)S(1)} %iota_compare_fusion.2), kind=kOutput, calls=%fused_computation.4 | convolution fusion | flops 402655232 | bytes 17826432 | tf_op jit(solution)/shard_map/bt,tif->bif/dot_general | solution.py:51
  171.7 20.7 %reduce-scatter.3.cloned.1.call-done = f32[256,256]{1,0:T(8,128)} async-done(((f32[1024,256]{1,0:T(8,128)}), f32[256,256]{1,0:T(8,128)}) %reduce-scatter.3.cloned.1.call-update) | async-done | bytes 262160 | tf_op jit(solution)/shard_map/reduce_scatter | solution.py:54
  195.7 24.6 %all-gather.5.cloned.1.call-done = f32[1024,256]{1,0:T(8,128)} async-done(((f32[256,256]{1,0:T(8,128)}), f32[1024,256]{1,0:T(8,128)}) %all-gather.5.cloned.1.call-update) | async-done | bytes 1048592 | tf_op jit(solution)/shard_map/all_gather | solution.py:63
  220.3 11.1 %gather_fusion.1 = f32[128,128,256]{2,1,0:T(8,128)} fusion(f32[8,128,256]{2,1,0:T(8,128)} %bitcast.51, s32[1024]{0:T(1024)S(1)} %pad_clamp_fusion), kind=kCustom, calls=%fused_computation.1 | custom fusion | bytes 33554944 | tf_op jit(solution)/shard_map/jit(_take)/gather | solution.py:64
  231.4 34.5 %fusion.4 = f32[128,256,128]{2,1,0:T(8,128)} fusion(f32[128,128,256]{2,1,0:T(8,128)} %gather_fusion.1, f32[1,1,128,128,128]{4,3,2,1,0:T(8,128)} %param.13, pred[128]{0:T(512)(128)(4,1)S(1)} %compare_and_fusion), kind=kOutput, calls=%fused_computation.6 | convolution fusion | flops 6446645248 | bytes 41943168 | tf_op jit(solution)/shard_map/tij,tif->tjf/dot_general | solution.py:65
  265.9 17.7 %copy.17 = f32[128,256,128]{1,0,2:T(8,128)} copy(f32[128,256,128]{2,1,0:T(8,128)} %fusion.4) | data formatting | bytes 33554432 | tf_op jit(solution)/shard_map/tij,tif->tjf/dot_general | solution.py:65
  283.6 9.9 %fusion = f32[40,128,256]{2,0,1:T(8,128)S(1)} fusion(f32[128,256,128]{1,0,2:T(8,128)} %copy.17, s32[128]{0:T(128)S(1)} %get-tuple-element.4, pred[128]{0:T(512)(128)(4,1)S(1)} %iota_compare_fusion.2), kind=kOutput, calls=%fused_computation.2 | convolution fusion | flops 2013276160 | bytes 22020736 | tf_op jit(solution)/shard_map/wt,tjf->wjf/dot_general | solution.py:69
  297.2 5.2 collective-permute-start.4
  302.4 2.7 collective-permute-start.5
  307.7 17.3 %collective-permute-done.4 = f32[1024,256]{1,0:T(8,128)} collective-permute-done((f32[1024,256]{1,0:T(8,128)}, f32[1024,256]{1,0:T(8,128)}, u32[]{:S(2)}, u32[]{:S(2)}) %collective-permute-start.4) | collective-permute-done | bytes 1048608 | tf_op jit(solution)/shard_map/ppermute | solution.py:14
  325.0 22.6 %collective-permute-done.5 = f32[1024,256]{1,0:T(8,128)} collective-permute-done((f32[1024,256]{1,0:T(8,128)}, f32[1024,256]{1,0:T(8,128)}, u32[]{:S(2)}, u32[]{:S(2)}) %collective-permute-start.5) | collective-permute-done | bytes 1048608 | tf_op jit(solution)/shard_map/ppermute | solution.py:14
  347.6 3.5 collective-permute-done.6
  351.1 3.5 collective-permute-done.7
  354.6 3.5 fusion.16
  358.1 224.1 %all-reduce.2.cloned.1.call-done = f32[256,256]{1,0:T(8,128)} async-done(((f32[256,256]{1,0:T(8,128)}), f32[256,256]{1,0:T(8,128)}) %all-reduce.2.cloned.1.call-update) | async-done | bytes 262160 | tf_op jit(solution)/shard_map/psum | solution.py:62
  582.2 26.5 %reduce-scatter.5.cloned.1.call-done = f32[256,256]{1,0:T(8,128)} async-done(((f32[1024,256]{1,0:T(8,128)}), f32[256,256]{1,0:T(8,128)}) %reduce-scatter.5.cloned.1.call-update) | async-done | bytes 262160 | tf_op jit(solution)/shard_map/reduce_scatter | solution.py:75
  (55 shorter events, 24.2 us)
Async XLA Ops:
  7.2 185.2 %copy-start = (f32[256,256]{1,0:T(8,128)S(1)}, f32[256,256]{1,0:T(8,128)}, u32[]{:S(2)}) copy-start(f32[256,256]{1,0:T(8,128)} %param.8) | copy-start | bytes 786436
  7.2 30.1 %all-gather.3.cloned.1.call-start = ((), (), s32[]{:S(2)}) async-start(), calls=%async_computation.2 | async-start | bytes 1310720 | tf_op jit(solution)/shard_map/all_gather | solution.py:40
  7.9 184.5 %reduce-scatter.3.cloned.1.call-start = ((), (), s32[]{:S(2)}) async-start(), calls=%async_computation.3 | async-start | bytes 1310720 | tf_op jit(solution)/shard_map/reduce_scatter | solution.py:54
  37.3 46.3 %collective-permute-start = (f32[1024,256]{1,0:T(8,128)}, f32[1024,256]{1,0:T(8,128)S(1)}, u32[]{:S(2)}, u32[]{:S(2)}) collective-permute-start(f32[1024,256]{1,0:T(8,128)} %all-gather.3.cloned.1.call-done), channel_id=1, source_target_pairs={{248,0},{252,4},{0,8},{4,12},{8,16},{12,20},{16,24},{20,28},{24,32... | collective-permute-start | bytes 3145736 | tf_op jit(solution)/shard_map/ppermute | solution.py:14
  38.5 52.2 %collective-permute-start.1 = (f32[1024,256]{1,0:T(8,128)}, f32[1024,256]{1,0:T(8,128)S(1)}, u32[]{:S(2)}, u32[]{:S(2)}) collective-permute-start(f32[1024,256]{1,0:T(8,128)} %all-gather.3.cloned.1.call-done), channel_id=1, source_target_pairs={{252,0},{0,4},{4,8},{8,12},{12,16},{16,20},{20,24},{24,28},{28,32}... | collective-permute-start | bytes 3145736 | tf_op jit(solution)/shard_map/ppermute | solution.py:14
  40.9 54.2 %collective-permute-start.3 = (f32[1024,256]{1,0:T(8,128)}, f32[1024,256]{1,0:T(8,128)S(1)}, u32[]{:S(2)}, u32[]{:S(2)}) collective-permute-start(f32[1024,256]{1,0:T(8,128)} %all-gather.3.cloned.1.call-done), channel_id=1, source_target_pairs={{8,0},{12,4},{16,8},{20,12},{24,16},{28,20},{32,24},{36,28},{40,32... | collective-permute-start | bytes 3145736 | tf_op jit(solution)/shard_map/ppermute | solution.py:14
  44.9 49.1 %collective-permute-start.2 = (f32[1024,256]{1,0:T(8,128)}, f32[1024,256]{1,0:T(8,128)S(1)}, u32[]{:S(2)}, u32[]{:S(2)}) collective-permute-start(f32[1024,256]{1,0:T(8,128)} %all-gather.3.cloned.1.call-done), channel_id=1, source_target_pairs={{4,0},{8,4},{12,8},{16,12},{20,16},{24,20},{28,24},{32,28},{36,32}... | collective-permute-start | bytes 3145736 | tf_op jit(solution)/shard_map/ppermute | solution.py:14
  143.2 17.7 %copy-start.2 = (s32[1,1,128]{2,1,0:T(1,128)S(1)}, s32[1,1,128]{2,1,0:T(1,128)}, u32[]{:S(2)}) copy-start(s32[1,1,128]{2,1,0:T(1,128)} %param.10) | copy-start | bytes 1540
  160.9 33.5 %copy-start.3 = (f32[256,256]{1,0:T(8,128)S(1)}, f32[256,256]{1,0:T(8,128)}, u32[]{:S(2)}) copy-start(f32[256,256]{1,0:T(8,128)} %param.9) | copy-start | bytes 786436
  171.4 48.9 %all-gather.5.cloned.1.call-start = ((), (), s32[]{:S(2)}) async-start(), calls=%async_computation.4 | async-start | bytes 1310720 | tf_op jit(solution)/shard_map/all_gather | solution.py:63
  194.4 37.0 %copy-start.6 = (f32[256,256]{1,0:T(8,128)}, f32[256,256]{1,0:T(8,128)S(1)}, u32[]{:S(2)}) copy-start(f32[256,256]{1,0:T(8,128)S(1)} %get-tuple-element.11) | copy-start | bytes 786436
  195.6 386.6 %all-reduce.2.cloned.1.call-start = ((), (), s32[]{:S(2)}) async-start(), calls=%async_computation.6 | async-start | bytes 524288 | tf_op jit(solution)/shard_map/psum | solution.py:62
  283.6 22.4 %copy-start.4 = (f32[256,256]{1,0:T(8,128)S(1)}, f32[256,256]{1,0:T(8,128)}, u32[]{:S(2)}) copy-start(f32[256,256]{1,0:T(8,128)} %param.9) | copy-start | bytes 786436
  283.6 22.4 %copy-start.5 = (f32[256,256]{1,0:T(8,128)S(1)}, f32[256,256]{1,0:T(8,128)}, u32[]{:S(2)}) copy-start(f32[256,256]{1,0:T(8,128)} %reduce-scatter.3.cloned.1.call-done) | copy-start | bytes 786436
  283.6 22.4 %copy-start.7 = (f32[256,256]{1,0:T(8,128)S(1)}, f32[256,256]{1,0:T(8,128)}, u32[]{:S(2)}) copy-start(f32[256,256]{1,0:T(8,128)} %copy-done.6) | copy-start | bytes 786436
  283.6 326.8 %copy-start.1 = (f32[256,256]{1,0:T(8,128)S(1)}, f32[256,256]{1,0:T(8,128)}, u32[]{:S(2)}) copy-start(f32[256,256]{1,0:T(8,128)} %param.8) | copy-start | bytes 786436
  297.2 27.8 %collective-permute-start.4 = (f32[1024,256]{1,0:T(8,128)}, f32[1024,256]{1,0:T(8,128)}, u32[]{:S(2)}, u32[]{:S(2)}) collective-permute-start(f32[1024,256]{1,0:T(8,128)} %bitcast.16), channel_id=1, source_target_pairs={{8,0},{12,4},{16,8},{20,12},{24,16},{28,20},{32,24},{36,28},{40,32... | collective-permute-start | bytes 3145736 | tf_op jit(solution)/shard_map/ppermute | solution.py:14
  302.4 45.2 %collective-permute-start.5 = (f32[1024,256]{1,0:T(8,128)}, f32[1024,256]{1,0:T(8,128)}, u32[]{:S(2)}, u32[]{:S(2)}) collective-permute-start(f32[1024,256]{1,0:T(8,128)} %bitcast.17), channel_id=1, source_target_pairs={{4,0},{8,4},{12,8},{16,12},{20,16},{24,20},{28,24},{32,28},{36,32}... | collective-permute-start | bytes 3145736 | tf_op jit(solution)/shard_map/ppermute | solution.py:14
  305.1 46.0 %collective-permute-start.6 = (f32[1024,256]{1,0:T(8,128)S(1)}, f32[1024,256]{1,0:T(8,128)}, u32[]{:S(2)}, u32[]{:S(2)}) collective-permute-start(f32[1024,256]{1,0:T(8,128)S(1)} %bitcast.54), channel_id=1, source_target_pairs={{252,0},{0,4},{4,8},{8,12},{12,16},{16,20},{20,24},{24,28},{28,32}... | collective-permute-start | bytes 3145736 | tf_op jit(solution)/shard_map/ppermute | solution.py:14
  305.4 49.2 %collective-permute-start.7 = (f32[1024,256]{1,0:T(8,128)S(1)}, f32[1024,256]{1,0:T(8,128)}, u32[]{:S(2)}, u32[]{:S(2)}) collective-permute-start(f32[1024,256]{1,0:T(8,128)S(1)} %bitcast.53), channel_id=1, source_target_pairs={{248,0},{252,4},{0,8},{4,12},{8,16},{12,20},{16,24},{20,28},{24,32... | collective-permute-start | bytes 3145736 | tf_op jit(solution)/shard_map/ppermute | solution.py:14
  307.4 301.4 %reduce-scatter.5.cloned.1.call-start = ((), (), s32[]{:S(2)}) async-start(), calls=%async_computation.5 | async-start | bytes 1310720 | tf_op jit(solution)/shard_map/reduce_scatter | solution.py:75
Sparse Core Ops, SparseCore 0:
  9.8 27.4 all-gather.2
  171.5 20.8 reduce-scatter.2
  195.7 24.5 all-gather.4
  307.5 274.6 all-reduce.1
  585.3 23.3 reduce-scatter.4
where the time goes:
time: 618 us; the launch traced here: 617 us
  waiting for transfers between devices  414 us (67%)
  matrix products  92.6 us (15%)
  local copies, waits for them, and re-layouts  72.6 us (12%)
  starting transfers between devices  18.3 us (3%)
  between operations  14.5 us (2%)
    psum x1, waiting for transfers between devices, shards(): weight_grad = lax.psum(local_wgrad, ('row', 'rep'))  224 us
    ppermute x8, waiting for transfers between devices, passed_along(): return lax.ppermute(block, axis, route)  88.1 us
    dot_general x1, matrix products, shards(): jnp.einsum('tij,tjf->tif', tile_vals, gathered, precision=precise)  34.5 us
    dot_general x1, matrix products, shards(): backward = jnp.einsum('tij,tif->tjf', tile_vals, picked, precision=precise)  34.5 us
    all_gather x1, waiting for transfers between devices, shards(): own_block = lax.all_gather(features, 'rep', axis=0, tiled=True)  29.3 us
    reduce_scatter x1, waiting for transfers between devices, shards(): lax.psum_scatter(summed, 'rep', scatter_dimension=0, tiled=True)  26.5 us
    all_gather x1, waiting for transfers between devices, shards(): lax.all_gather(grad_agg, 'rep', axis=0, tiled=True)  24.6 us
    reduce_scatter x1, waiting for transfers between devices, shards(): lax.psum_scatter(partial_value, 'rep', scatter_dimension=0, tiled=True)  20.7 us
  transfers between devices with their start and end apart: 13, of which 11 were waited for; matrix products, arithmetic and copies ran while one was open for 2% of the time, Pallas kernels for 0%

commit v1 on v0

v1 whole, which is shorter than its diff:
```python
import jax
import jax.numpy as jnp
from jax import lax
from jax.experimental import pallas as pl
from jax.experimental.pallas import tpu as pltpu
from jax.sharding import PartitionSpec as P

TILE = 128
TPB = 8
SPAN = 2
SLOTS = 128
F = 256
ROWS = 256
WIN = 20
BAND_TILES = 40
PLANE = 32
MESH = pl.DeviceIdType.MESH
F32 = jnp.float32
BF16 = jnp.bfloat16


def split(value):
    high = value.astype(BF16)
    low = (value - high.astype(F32)).astype(BF16)
    return high, low


def dot(a, b):
    return jnp.dot(a, b, preferred_element_type=F32)


def dot_t(a, b):
    return lax.dot_general(a, b, (((1,), (1,)), ((), ())), preferred_element_type=F32)


def dot3(op, a, b):
    ah, al = split(a)
    bh, bl = split(b)
    return op(ah, bh) + (op(al, bh) + op(ah, bl))


def choose(i, values):
    out = values[0]
    for k in range(1, len(values)):
        out = jnp.where(i == k, values[k], out)
    return out


def kernel(
    feat, weight, cot, tiles, perm, keep, place,
    act_out, fg_out, wg_out,
    tilebuf, run, dense_h, dense_l, win, acc, rs_in, rs_mid, rs_send, gt, gt_h, gt_l, mrecv, rbuf,
    wg_loc, ar_a, ar_b, wg_sum, cot_v, w_v,
    loc_sem, fs_sem, fr_sem, ms_sem, mr_sem, rs_s, rs_r, ag_s, ag_r, bm_s, bm_r, br_s, br_r,
    aa_s, aa_r, ab_s, ab_r, ac_s, ac_r,
):
    row = lax.axis_index("row")
    rep = lax.axis_index("rep")
    yy = lax.div(row, 2)
    xl = lax.div(rep, 2)
    c = lax.rem(rep, 2)
    xh = lax.rem(row, 2)
    x = xh * 2 + xl
    q = x + 1 - 2 * xl
    w = 3 - x
    o = lax.rem(x + 2, 4)
    h = 2 * xh - 1
    l = 1 - 2 * xh
    nyy = lax.axis_size("row") // 2

    def dev(xx, yv, cc):
        yv = lax.rem(yv + nyy, nyy)
        return (yv * 2 + lax.div(xx, 2), lax.rem(xx, 2) * 2 + cc)

    def slot(at, dyy, xx, cc):
        return (2 * dyy + lax.div(xx, 2) - lax.div(at, 2) + SPAN) * 4 + lax.rem(xx, 2) * 2 + cc

    mate = dev(x, yy, 1 - c)
    zi = lax.div(row, 8)
    nz = nyy // 4
    m_me = lax.rem(row, 8) * 4 + rep

    def plane_dev(m):
        return (zi * 8 + lax.div(m, 4), lax.rem(m, 4))

    def remote(src, dst, ssem, rsem, to):
        return pltpu.make_async_remote_copy(
            src_ref=src, dst_ref=dst, send_sem=ssem, recv_sem=rsem, device_id=to, device_id_type=MESH
        )

    tile_cp = pltpu.make_async_copy(tiles, tilebuf, loc_sem.at[0])
    tile_cp.start()
    own = slot(x, 0, x, c)
    feat_cp = pltpu.make_async_copy(feat, win.at[own], loc_sem.at[1])
    feat_cp.start()
    cot_cp = pltpu.make_async_copy(cot, cot_v, loc_sem.at[2])
    cot_cp.start()
    w_cp = pltpu.make_async_copy(weight, w_v, loc_sem.at[3])
    w_cp.start()

    bar = pltpu.get_barrier_semaphore()

    def greet(to):
        pl.semaphore_signal(bar, inc=1, device_id=to, device_id_type=MESH)

    @pl.loop(1, PLANE)
    def _(d):
        greet(plane_dev(lax.rem(m_me + d, PLANE)))

    @pl.loop(1, nz)
    def _(d):
        greet((lax.rem(row + 8 * d, nz * 8), rep))

    greet(dev(x, yy + 1, c))
    greet(dev(x, yy - 1, c))
    pl.semaphore_wait(bar, PLANE - 1 + nz - 1 + 2)

    sends = []

    def fsend(n, src, dst_slot, to):
        cp = remote(src, win.at[dst_slot], fs_sem.at[n], fr_sem.at[dst_slot], to)
        cp.start()
        sends.append(cp)

    def frecv(s):
        remote(feat, win.at[s], fs_sem.at[0], fr_sem.at[s], mate).wait_recv()

    fsend(0, feat, slot(q, 0, x, c), dev(q, yy, c))
    fsend(1, feat, slot(x, -1, x, c), dev(x, yy + 1, c))
    fsend(2, feat, slot(x, 1, x, c), dev(x, yy - 1, c))
    fsend(3, feat, slot(w, 0, x, c), dev(w, yy, c))
    fsend(4, feat, own, mate)

    acc[...] = jnp.zeros_like(acc)
    run[SLOTS] = jnp.zeros((TILE, TILE), F32)
    tile_cp.wait()

    def merge(t, prev):
        value = prev * keep[t] + tilebuf[perm[t]]
        run[t] = value
        return value

    lax.fori_loop(0, SLOTS, merge, jnp.zeros((TILE, TILE), F32))

    @pl.loop(0, WIN)
    def _(j):
        for r in range(TPB):
            for half in range(2):
                high, low = split(run[place[r * BAND_TILES + j * 2 + half]])
                dense_h[j, r * TILE:(r + 1) * TILE, half * TILE:(half + 1) * TILE] = high
                dense_l[j, r * TILE:(r + 1) * TILE, half * TILE:(half + 1) * TILE] = low

    feat_cp.wait()

    def forward(s):
        xh_, xl_ = split(win[s])
        a = dense_h[s]
        acc[...] += dot(a, xh_) + (dot(dense_l[s], xh_) + dot(a, xl_))

    def forward_group(slots):
        @pl.loop(0, len(slots))
        def _(i):
            forward(choose(i, slots))

    def forward_recv_group(slots):
        @pl.loop(0, len(slots))
        def _(i):
            s = choose(i, slots)
            frecv(s)
            forward(s)

    def flip(s):
        return s + 1 - 2 * c

    s_q, s_w = slot(x, 0, q, c), slot(x, 0, w, c)
    s_hx, s_lx = slot(x, h, x, c), slot(x, l, x, c)
    s_o, s_hw = slot(x, 0, o, c), slot(x, h, w, c)
    s_lq, s_hq = slot(x, l, q, c), slot(x, h, q, c)
    s_ho = slot(x, h, o, c)

    frecv(s_q)
    fsend(5, win.at[s_q], slot(w, 0, q, c), dev(w, yy, c))
    fsend(6, win.at[s_q], slot(x, l, q, c), dev(x, yy + h, c))
    frecv(s_w)
    fsend(7, win.at[s_w], slot(x, h, w, c), dev(x, yy - h, c))
    frecv(s_hx)
    qh_src = jnp.where(c == 0, s_hx, s_q)
    qh_dst = jnp.where(c == 0, slot(q, h, x, c), slot(x, h, q, c))
    to_q, to_y = dev(q, yy, c), dev(x, yy - h, c)
    qh_to = (jnp.where(c == 0, to_q[0], to_y[0]), jnp.where(c == 0, to_q[1], to_y[1]))
    fsend(8, win.at[qh_src], qh_dst, qh_to)
    frecv(s_lx)
    fsend(9, win.at[s_q], s_q, mate)
    fsend(10, win.at[s_w], s_w, mate)
    fsend(11, win.at[s_hx], s_hx, mate)
    fsend(12, win.at[s_lx], s_lx, mate)
    forward_group([own, s_q, s_w])
    frecv(s_hw)
    fsend(13, win.at[s_hw], slot(q, h, w, c), dev(q, yy, c))
    fsend(14, win.at[s_hw], s_hw, mate)
    forward_group([s_hx, s_lx])
    frecv(s_o)
    fsend(15, win.at[s_o], s_o, mate)
    frecv(s_lq)
    fsend(16, win.at[s_lq], s_lq, mate)
    frecv(s_hq)
    fsend(17, win.at[s_hq], s_hq, mate)
    forward_recv_group([flip(own), flip(s_q), flip(s_w), flip(s_hx), flip(s_lx), flip(s_hw)])
    forward_group([s_hw, s_o, s_lq, s_hq])
    frecv(s_ho)
    fsend(18, win.at[s_ho], s_ho, mate)
    forward_recv_group([flip(s_o), flip(s_lq), flip(s_hq)])
    forward_group([s_ho])
    forward_recv_group([flip(s_ho)])

    k_o = (1 - xl) * 2 + c
    k_m = xl * 2 + 1 - c
    k_mo = (1 - xl) * 2 + 1 - c

    def chunk(k):
        return acc.at[pl.ds(pl.multiple_of(k * ROWS, ROWS), ROWS)]

    rs0 = remote(chunk(k_mo), rs_in.at[0], rs_s.at[0], rs_r.at[0], mate)
    rs0.start()
    rs1 = remote(chunk(k_m), rs_in.at[1], rs_s.at[1], rs_r.at[1], mate)
    rs1.start()
    for cp in sends:
        cp.wait_send()
    cot_cp.wait()
    w_cp.wait()
    rs0.wait_recv()
    rs_send[...] = chunk(k_o)[...] + rs_in[0]
    rs2 = remote(rs_send, rs_mid, rs_s.at[2], rs_r.at[2], dev(q, yy, c))
    rs2.start()
    rs1.wait_recv()
    rs2.wait_recv()
    agg = chunk(rep)[...] + rs_in[1] + rs_mid[...]

    wv = w_v[...]
    pre = dot3(dot, agg, wv)
    sig = jax.nn.sigmoid(pre)
    act_out[...] = pre * sig
    gp = cot_v[...] * (sig * (1.0 + pre * (1.0 - sig)))
    gt[rep] = dot3(dot_t, wv, gp)

    ag0 = remote(gt.at[rep], gt.at[rep], ag_s.at[0], ag_r.at[rep], dev(q, yy, c))
    ag0.start()
    ag1 = remote(gt.at[rep], gt.at[rep], ag_s.at[1], ag_r.at[rep], mate)
    ag1.start()

    def grecv(k):
        remote(gt.at[k], gt.at[k], ag_s.at[0], ag_r.at[k], mate).wait_recv()

    wg = dot3(dot, agg.T, gp).reshape(PLANE, F // PLANE, F)
    wg_loc[...] = wg

    def ar_copy(d, src, dst, ssem, rsem):
        return remote(src, dst, ssem.at[d], rsem.at[d], plane_dev(lax.rem(m_me + d, PLANE)))

    def aa_copy(d):
        return ar_copy(d, wg_loc.at[lax.rem(m_me + d, PLANE)], ar_a.at[m_me], aa_s, aa_r)

    def ab_copy(d):
        return remote(wg_sum, ar_b.at[zi], ab_s.at[d], ab_r.at[d], (lax.rem(row + 8 * d, nz * 8), rep))

    def ac_copy(d):
        return ar_copy(d, wg_out.at[m_me], wg_out.at[m_me], ac_s, ac_r)

    @pl.loop(1, PLANE)
    def _(d):
        aa_copy(d).start()

    ar_a[m_me] = wg_loc[m_me]

    grecv(k_m)

    def spread(pair):
        for half in range(2):
            high, low = split(gt[pair * 2 + half])
            gt_h[pair, :, half * ROWS:(half + 1) * ROWS] = high
            gt_l[pair, :, half * ROWS:(half + 1) * ROWS] = low

    def backward(s, pair):
        rows = pl.ds(pl.multiple_of(pair * 2 * ROWS, 2 * ROWS), 2 * ROWS)
        a = dense_h[s, rows, :]
        g = gt_h[pair]
        return dot(g, a) + (dot(gt_l[pair], a) + dot(g, dense_l[s, rows, :]))

    spread(xl)

    def first_pass(begin, end):
        @pl.loop(begin, end)
        def _(s):
            win[s] = backward(s, xl)

    first_pass(0, 12)
    grecv(k_o)
    ag2 = remote(gt.at[k_o], gt.at[k_o], ag_s.at[2], ag_r.at[k_o], mate)
    ag2.start()

    @pl.loop(1, PLANE)
    def _(d):
        aa_copy(d).wait_recv()

    total = ar_a[0]
    for k in range(1, PLANE):
        total = total + ar_a[k]
    wg_sum[...] = total
    ar_b[zi] = total

    @pl.loop(1, nz)
    def _(d):
        ab_copy(d).start()

    first_pass(12, WIN)
    grecv(k_mo)
    spread(1 - xl)

    @pl.loop(1, nz)
    def _(d):
        ab_copy(d).wait_recv()

    total = ar_b[0]
    for k in range(1, nz):
        total = total + ar_b[k]
    wg_out[m_me] = total

    @pl.loop(1, PLANE)
    def _(d):
        ac_copy(d).start()

    def mate_copy(s):
        i = lax.div(s, 2)
        return remote(win.at[s], mrecv.at[i], bm_s.at[i], bm_r.at[i], mate)

    def second_pass(slots):
        @pl.loop(0, len(slots))
        def _(i):
            s = choose(i, slots)
            other = flip(s)
            win[other] += backward(other, 1 - xl)
            mate_copy(other).start()
            win[s] += backward(s, 1 - xl)

    def add_mate(s):
        mate_copy(s).wait_recv()
        win[s] += mrecv[lax.div(s, 2)]

    back = []

    def bsend(n, s, to):
        cp = remote(win.at[s], rbuf.at[n], br_s.at[n], br_r.at[n], to)
        cp.start()
        back.append(cp)

    def badd(n, s):
        back[n].wait_recv()
        win[s] += rbuf[n]

    second_pass([s_ho, s_o, s_lq])
    add_mate(s_ho)
    bsend(0, s_ho, dev(q, yy, c))
    second_pass([s_hq, s_hw])
    add_mate(s_o)
    bsend(1, s_o, dev(w, yy, c))
    add_mate(s_lq)
    bsend(2, s_lq, dev(x, yy + l, c))
    add_mate(s_hq)
    from_q, from_y = dev(q, yy, c), dev(x, yy + h, c)
    hq_to = (jnp.where(c == 0, from_q[0], from_y[0]), jnp.where(c == 0, from_q[1], from_y[1]))
    bsend(3, s_hq, hq_to)
    second_pass([s_q, s_w, s_hx, s_lx])
    add_mate(s_hw)
    badd(0, s_hw)
    bsend(4, s_hw, dev(x, yy + h, c))
    second_pass([own])
    add_mate(s_q)
    add_mate(s_w)
    add_mate(s_hx)
    add_mate(s_lx)
    add_mate(own)
    bsend(5, s_lx, dev(x, yy + l, c))
    badd(1, s_q)
    badd(2, s_q)
    badd(3, jnp.where(c == 0, s_hx, s_q))
    bsend(6, s_q, dev(q, yy, c))
    bsend(7, s_hx, dev(x, yy + h, c))
    badd(4, s_w)
    bsend(8, s_w, dev(w, yy, c))
    for n in (5, 6, 7, 8):
        back[n].wait_recv()
    fg_out[...] = (win[own] + rbuf[5] + rbuf[6] + rbuf[7] + rbuf[8]).T

    @pl.loop(1, PLANE)
    def _(d):
        ac_copy(d).wait_recv()

    for cp in back + [rs0, rs1, rs2, ag0, ag1, ag2]:
        cp.wait_send()
    for i in range(WIN // 2):
        mate_copy(2 * i + 1 - c).wait_send()

    @pl.loop(1, PLANE)
    def _(d):
        aa_copy(d).wait_send()
        ac_copy(d).wait_send()

    @pl.loop(1, nz)
    def _(d):
        ab_copy(d).wait_send()


def shards(features, weight, cotangent, tile_row, tile_col, tile_count, tile_values):
    tile_rows = tile_row[0, 0]
    tile_cols = tile_col[0, 0]
    slot_ids = jnp.arange(SLOTS, dtype=jnp.int32)
    live = slot_ids < tile_count[0, 0]
    row_index = lax.axis_index("row")
    total_tiles = TPB * lax.axis_size("row")
    position = jnp.mod(tile_cols - (row_index - SPAN) * TPB, total_tiles)
    places = TPB * BAND_TILES
    key = jnp.where(live, tile_rows * BAND_TILES + position, places + slot_ids)
    before = (key[None, :] < key[:, None]) | ((key[None, :] == key[:, None]) & (slot_ids[None, :] < slot_ids[:, None]))
    rank = jnp.sum(before.astype(jnp.int32), axis=1)
    hit = rank[None, :] == slot_ids[:, None]
    perm = jnp.sum(jnp.where(hit, slot_ids[None, :], 0), axis=1)
    first = ~jnp.any((key[None, :] == key[:, None]) & (slot_ids[None, :] < slot_ids[:, None]), axis=1)
    keep = jnp.sum(jnp.where(hit & ~first[None, :], 1.0, 0.0), axis=1)
    spots = jnp.arange(places, dtype=jnp.int32)
    upto = jnp.sum((key[None, :] <= spots[:, None]).astype(jnp.int32), axis=1)
    there = jnp.any(key[None, :] == spots[:, None], axis=1)
    place = jnp.where(there, upto - 1, SLOTS)

    nz = lax.axis_size("row") // 8
    smem = pl.BlockSpec(memory_space=pltpu.SMEM)
    vmem = pl.BlockSpec(memory_space=pltpu.VMEM)
    anywhere = pl.BlockSpec(memory_space=pl.ANY)
    sem = pltpu.SemaphoreType.DMA
    act, fg, wg = pl.pallas_call(
        kernel,
        out_shape=(
            jax.ShapeDtypeStruct((ROWS, F), F32),
            jax.ShapeDtypeStruct((ROWS, F), F32),
            jax.ShapeDtypeStruct((PLANE, F // PLANE, F), F32),
        ),
        in_specs=[anywhere, anywhere, anywhere, anywhere, smem, smem, smem],
        out_specs=(vmem, vmem, vmem),
        scratch_shapes=[
            pltpu.VMEM((SLOTS, TILE, TILE), F32),
            pltpu.VMEM((SLOTS + 1, TILE, TILE), F32),
            pltpu.VMEM((WIN, TPB * TILE, 2 * TILE), BF16),
            pltpu.VMEM((WIN, TPB * TILE, 2 * TILE), BF16),
            pltpu.VMEM((WIN, ROWS, F), F32),
            pltpu.VMEM((4 * ROWS, F), F32),
            pltpu.VMEM((2, ROWS, F), F32),
            pltpu.VMEM((ROWS, F), F32),
            pltpu.VMEM((ROWS, F), F32),
            pltpu.VMEM((4, F, ROWS), F32),
            pltpu.VMEM((2, F, 2 * ROWS), BF16),
            pltpu.VMEM((2, F, 2 * ROWS), BF16),
            pltpu.VMEM((WIN // 2, F, ROWS), F32),
            pltpu.VMEM((9, F, ROWS), F32),
            pltpu.VMEM((PLANE, F // PLANE, F), F32),
            pltpu.VMEM((PLANE, F // PLANE, F), F32),
            pltpu.VMEM((nz, F // PLANE, F), F32),
            pltpu.VMEM((F // PLANE, F), F32),
            pltpu.VMEM((ROWS, F), F32),
            pltpu.VMEM((F, F), F32),
            sem((4,)), sem((19,)), sem((WIN,)), sem((1,)), sem((1,)), sem((3,)), sem((3,)), sem((3,)), sem((4,)),
            sem((WIN // 2,)), sem((WIN // 2,)), sem((9,)), sem((9,)),
            sem((PLANE,)), sem((PLANE,)), sem((nz,)), sem((nz,)), sem((PLANE,)), sem((PLANE,)),
        ],
        compiler_params=pltpu.CompilerParams(
            collective_id=0, has_side_effects=True, vmem_limit_bytes=62 * 1024 * 1024
        ),
    )(features, weight, cotangent, tile_values[0, 0], perm, keep, place)
    return act, fg, wg.reshape(F, F)


def solution(mesh):
    placed = (
        P(("row", "rep"), None),
        P(),
        P(("row", "rep"), None),
        P("row", "rep", None),
        P("row", "rep", None),
        P("row", "rep"),
        P("row", "rep", None, None, None),
    )
    return jax.shard_map(
        shards,
        mesh=mesh,
        in_specs=placed,
        out_specs=(P(("row", "rep"), None), P(("row", "rep"), None), P()),
        check_vma=False,
    )
```

time: 618 us -> 105 us (0.17)
  waiting for transfers between devices: 414 us -> 0 us
  Pallas kernels: 0 us -> 94.5 us
  matrix products: 92.6 us -> 0 us
  local copies, waits for them, and re-layouts: 72.6 us -> 5.01 us
  starting transfers between devices: 18.3 us -> 0 us
  between operations: 14.5 us -> 1.3 us
    psum x1 -> x0, waiting for transfers between devices: 224 us -> none  [shards(): weight_grad = lax.psum(local_wgrad, ('row', 'rep'))]
    pallas_call x0 -> x1, Pallas kernels: none -> 94.5 us  [shards(): pl.pallas_call(kernel, out_shape=(jax.ShapeDtypeStruct((ROWS, F), F32), j...]
    dot_general x7 -> x0, matrix products: 92.6 us -> none  [the longest x1 34.5 us: shards(): jnp.einsum('tij,tjf->tif', tile_vals, gathered, precision=precise)]
    ppermute x8 -> x0, waiting for transfers between devices: 88.1 us -> none  [passed_along(): return lax.ppermute(block, axis, route)]
    all_gather x2 -> x0, waiting for transfers between devices: 54 us -> none  [the longest x1 29.3 us: shards(): own_block = lax.all_gather(features, 'rep', axis=0, tiled=True)]
    reduce_scatter x2 -> x0, waiting for transfers between devices: 47.2 us -> none  [the longest x1 26.5 us: shards(): lax.psum_scatter(summed, 'rep', scatter_dimension=0, tiled=True)]
    dot_general x3 -> x0, local copies, waits for them, and re-layouts: 36.7 us -> none  [the longest x1 17.7 us: shards(): jnp.einsum('tij,tjf->tif', tile_vals, gathered, precision=precise)]
    gather x2 -> x0, local copies, waits for them, and re-layouts: 23.6 us -> none  [the longest x1 12.5 us: shards(): gathered = jnp.take(window, position, axis=0)]
  transfers between devices with their start and end apart: 13 -> 0, of which waited for: 11 -> 0; matrix products, arithmetic and copies ran while one was open for 2% -> 0% of each run, Pallas kernels for 0% -> 0%
where the time goes in v1:
time: 105 us; the launch traced here: 104 us
  Pallas kernels  94.5 us (90%)
  local copies, waits for them, and re-layouts  5.01 us (5%)
  other arithmetic  3.19 us (3%)
  between operations  1.3 us (1%)
    pallas_call x1, Pallas kernels, shards(): pl.pallas_call(kernel, out_shape=(jax.ShapeDtypeStruct((ROWS, F), F32), j...  94.5 us
    unnamed x3, local copies, waits for them, and re-layouts  5.01 us

profile of v1, /device:TPU:1, one launch (start us, length us, event | category | flops | bytes accessed | tf_op | source)
XLA Modules:
  0.0 104.0 jit_solution(16838374631140330673)
XLA Ops:
  1.3 0.7 compare_select_fusion.2
  2.0 0.2 convert_reduce_fusion.1
  2.1 0.6 select_reduce_fusion.1.perm
  2.8 0.1 fusion
  2.9 0.2 fusion.3
  3.1 0.6 select_reduce_fusion.keep
  3.7 0.1 convert_reduce_fusion
  3.9 0.6 add_select_fusion.place
  4.5 94.5 %shard_map.94 = (f32[256,256]{1,0:T(8,128)}, f32[256,256]{1,0:T(8,128)}, f32[32,8,256]{2,1,0:T(8,128)}) custom-call(f32[256,256]{1,0:T(8,128)} %feat.1, f32[256,256]{1,0:T(8,128)} %weight.1, f32[256,256]{1,0:T(8,128)} %cot.1, f32[128,128,128]{2,1,0:T(8,128)} %bitcast.8, s32[128]{0:T(128)} %select_reduce_fusion.1.perm, f32[128]{0:T(128)} %select_reduce_fusion.keep, ...), custom_call_target="tpu_custom_call" | custom-call | tf_op jit(solution)/shard_map/pallas_call | solution.py:439
  99.0 1.7 %copy.14 = f32[256,256]{1,0:T(8,128)} copy(f32[256,256]{1,0:T(8,128)} %get-tuple-element.12) | data formatting | bytes 524288
  100.7 1.7 %copy.15 = f32[256,256]{1,0:T(8,128)} copy(f32[256,256]{1,0:T(8,128)} %get-tuple-element.13) | data formatting | bytes 524288
  102.4 1.7 %copy.16 = f32[256,256]{1,0:T(8,128)} copy(f32[256,256]{1,0:T(8,128)} %bitcast.9) | data formatting | bytes 524288

commit v2 on v1

v2 whole, which is shorter than its diff:
```python
import jax
import jax.numpy as jnp
from jax import lax
from jax.experimental import pallas as pl
from jax.experimental.pallas import tpu as pltpu
from jax.sharding import PartitionSpec as P

TILE = 128
TPB = 8
SPAN = 2
SLOTS = 128
F = 256
ROWS = 256
WIN = 20
BAND_TILES = 40
PLANE = 32
PARTS_F = 2
PARTS_B = 4
HALF = 128
MESH = pl.DeviceIdType.MESH
F32 = jnp.float32
BF16 = jnp.bfloat16


def split(value):
    high = value.astype(BF16)
    low = (value - high.astype(F32)).astype(BF16)
    return high, low


def dot(a, b):
    return jnp.dot(a, b, preferred_element_type=F32)


def dot_t(a, b):
    return lax.dot_general(a, b, (((1,), (1,)), ((), ())), preferred_element_type=F32)


def dot3(op, a, b):
    ah, al = split(a)
    bh, bl = split(b)
    return op(ah, bh) + (op(al, bh) + op(ah, bl))


def choose(i, values):
    out = values[0]
    for k in range(1, len(values)):
        out = jnp.where(i == k, values[k], out)
    return out


def plan_tiles(row, total_tiles, rows, cols, count, plan):
    sub = lax.broadcasted_iota(jnp.int32, (SLOTS, SLOTS), 0)
    lane = lax.broadcasted_iota(jnp.int32, (SLOTS, SLOTS), 1)
    line = lax.broadcasted_iota(jnp.int32, (1, SLOTS), 1)

    def total(mask_or_value):
        return jnp.sum(mask_or_value, axis=0, keepdims=True)

    def ones(mask):
        return jnp.where(mask, 1, 0)

    position = cols - (row - SPAN) * TPB
    position = jnp.where(position < 0, position + total_tiles, position)
    position = jnp.where(position >= total_tiles, position - total_tiles, position)
    key = jnp.where(line < count, rows * BAND_TILES + position, TPB * BAND_TILES + line)
    key_r = jnp.broadcast_to(key, (SLOTS, SLOTS))
    key_c = key_r.T
    twin = ones((key_c == key_r) & (sub < lane))
    rank = total(ones(key_c < key_r) + twin)
    again = jnp.minimum(total(twin), 1)
    code = jnp.broadcast_to(rank * 2 + again, (SLOTS, SLOTS)).T
    again_c = code & 1
    hit = code - again_c == lane * 2
    plan[0:1, :] = total(jnp.where(hit, sub, 0))
    plan[1:2, :] = total(jnp.where(hit, again_c, 0))
    for part in range(3):
        spot = lane + part * SLOTS
        upto = total(ones(key_c <= spot))
        there = total(ones(key_c == spot))
        plan[2 + part:3 + part, :] = jnp.where(there > 0, upto - 1, SLOTS)


def deliver(act, fg, wg, act_out, fg_out, wg_out, stage, sem_in, sem_out):
    pairs = ((act, act_out), (fg, fg_out), (wg, wg_out))
    inward = [pltpu.make_async_copy(src, stage.at[i], sem_in.at[i]) for i, (src, _) in enumerate(pairs)]
    outward = [pltpu.make_async_copy(stage.at[i], dst, sem_out.at[i]) for i, (_, dst) in enumerate(pairs)]
    for cp in inward:
        cp.start()
    for cp, onward in zip(inward, outward):
        cp.wait()
        onward.start()
    for cp in outward:
        cp.wait()


def kernel(
    feat, weight, cot, tiles, tile_row, tile_col, tile_count,
    act_out, fg_out, wg_out,
    tilebuf, run, dense_h, dense_l, win, acc, rs_in, rs_mid, rs_send, gt, gt_h, gt_l, mrecv, rbuf,
    wg_loc, ar_a, ar_b, wg_sum, wg_all, cot_v, w_v, row_v, col_v, count_v, plan_v, plan,
    loc_sem, fs_sem, fr_sem, rs_s, rs_r, ag_s, ag_r, bm_s, bm_r, br_s, br_r,
    aa_s, aa_r, ab_s, ab_r, ac_s, ac_r,
):
    row = lax.axis_index("row")
    rep = lax.axis_index("rep")
    yy = lax.div(row, 2)
    xl = lax.div(rep, 2)
    c = lax.rem(rep, 2)
    xh = lax.rem(row, 2)
    x = xh * 2 + xl
    q = x + 1 - 2 * xl
    w = 3 - x
    o = lax.rem(x + 2, 4)
    h = 2 * xh - 1
    l = 1 - 2 * xh
    nyy = lax.axis_size("row") // 2

    def dev(xx, yv, cc):
        yv = lax.rem(yv + nyy, nyy)
        return (yv * 2 + lax.div(xx, 2), lax.rem(xx, 2) * 2 + cc)

    def slot(at, dyy, xx, cc):
        return (2 * dyy + lax.div(xx, 2) - lax.div(at, 2) + SPAN) * 4 + lax.rem(xx, 2) * 2 + cc

    mate = dev(x, yy, 1 - c)
    zi = lax.div(row, 8)
    nz = nyy // 4
    m_me = lax.rem(row, 8) * 4 + rep

    def plane_dev(m):
        return (zi * 8 + lax.div(m, 4), lax.rem(m, 4))

    def remote(src, dst, ssem, rsem, to):
        return pltpu.make_async_remote_copy(
            src_ref=src, dst_ref=dst, send_sem=ssem, recv_sem=rsem, device_id=to, device_id_type=MESH
        )

    tile_cp = pltpu.make_async_copy(tiles, tilebuf, loc_sem.at[0])
    tile_cp.start()
    own = slot(x, 0, x, c)
    feat_cp = pltpu.make_async_copy(feat, win.at[own], loc_sem.at[1])
    feat_cp.start()
    cot_cp = pltpu.make_async_copy(cot, cot_v, loc_sem.at[2])
    cot_cp.start()
    w_cp = pltpu.make_async_copy(weight, w_v, loc_sem.at[3])
    w_cp.start()
    list_cps = [
        pltpu.make_async_copy(src, dst, loc_sem.at[4 + i])
        for i, (src, dst) in enumerate(((tile_row, row_v), (tile_col, col_v), (tile_count, count_v)))
    ]
    for cp in list_cps:
        cp.start()

    bar = pltpu.get_barrier_semaphore()

    def greet(to):
        pl.semaphore_signal(bar, inc=1, device_id=to, device_id_type=MESH)

    @pl.loop(1, PLANE)
    def _(d):
        greet(plane_dev(lax.rem(m_me + d, PLANE)))

    @pl.loop(1, nz)
    def _(d):
        greet((lax.rem(row + 8 * d, nz * 8), rep))

    greet(dev(x, yy + 1, c))
    greet(dev(x, yy - 1, c))
    pl.semaphore_wait(bar, PLANE - 1 + nz - 1 + 2)

    sends = []

    def piece(k, parts):
        return pl.ds(k * (ROWS // parts), ROWS // parts)

    def fsend(n, k, src, dst_slot, to):
        part = piece(k, PARTS_F)
        cp = remote(src.at[part], win.at[dst_slot, part], fs_sem.at[n, k], fr_sem.at[dst_slot, k], to)
        cp.start()
        sends.append(cp)

    def frecv(s, k):
        part = piece(k, PARTS_F)
        remote(feat.at[part], win.at[s, part], fs_sem.at[0, k], fr_sem.at[s, k], mate).wait_recv()

    for k in range(PARTS_F):
        fsend(1, k, feat, slot(x, -1, x, c), dev(x, yy + 1, c))
        fsend(2, k, feat, slot(x, 1, x, c), dev(x, yy - 1, c))
        fsend(0, k, feat, slot(q, 0, x, c), dev(q, yy, c))
        fsend(3, k, feat, slot(w, 0, x, c), dev(w, yy, c))
    for k in range(PARTS_F):
        fsend(4, k, feat, own, mate)

    acc[...] = jnp.zeros_like(acc)
    run[SLOTS] = jnp.zeros((TILE, TILE), F32)
    for cp in list_cps:
        cp.wait()
    plan_tiles(row, nyy * 2 * TPB, row_v[0], col_v[0], count_v[...], plan_v)
    plan_cp = pltpu.make_async_copy(plan_v, plan, loc_sem.at[7])
    plan_cp.start()
    plan_cp.wait()
    tile_cp.wait()

    def merge(t, prev):
        value = prev * plan[1, t].astype(F32) + tilebuf[plan[0, t]]
        run[t] = value
        return value

    lax.fori_loop(0, SLOTS, merge, jnp.zeros((TILE, TILE), F32))

    feat_cp.wait()

    def forward(s):
        for r in range(TPB):
            for half in range(2):
                spot = s * 2 + (r * BAND_TILES + half)
                high, low = split(run[plan[2 + lax.div(spot, SLOTS), lax.rem(spot, SLOTS)]])
                dense_h[s, r * TILE:(r + 1) * TILE, half * TILE:(half + 1) * TILE] = high
                dense_l[s, r * TILE:(r + 1) * TILE, half * TILE:(half + 1) * TILE] = low
        xh_, xl_ = split(win[s])
        a = dense_h[s]
        acc[...] += dot(a, xh_) + (dot(dense_l[s], xh_) + dot(a, xl_))

    def forward_group(slots):
        @pl.loop(0, len(slots))
        def _(i):
            forward(choose(i, slots))

    def forward_recv_group(slots):
        @pl.loop(0, len(slots))
        def _(i):
            s = choose(i, slots)
            for k in range(PARTS_F):
                frecv(s, k)
            forward(s)

    def flip(s):
        return s + 1 - 2 * c

    s_q, s_w = slot(x, 0, q, c), slot(x, 0, w, c)
    s_hx, s_lx = slot(x, h, x, c), slot(x, l, x, c)
    s_o, s_hw = slot(x, 0, o, c), slot(x, h, w, c)
    s_lq, s_hq = slot(x, l, q, c), slot(x, h, q, c)
    s_ho = slot(x, h, o, c)

    qh_src = jnp.where(c == 0, s_hx, s_q)
    qh_dst = jnp.where(c == 0, slot(q, h, x, c), slot(x, h, q, c))
    to_q, to_y = dev(q, yy, c), dev(x, yy - h, c)
    qh_to = (jnp.where(c == 0, to_q[0], to_y[0]), jnp.where(c == 0, to_q[1], to_y[1]))

    def relay(n, k, s):
        frecv(s, k)
        fsend(n, k, win.at[s], s, mate)

    forward_group([own])
    for k in range(PARTS_F):
        frecv(s_w, k)
        fsend(7, k, win.at[s_w], slot(x, h, w, c), dev(x, yy - h, c))
        frecv(s_q, k)
        fsend(6, k, win.at[s_q], slot(x, l, q, c), dev(x, yy + h, c))
        fsend(5, k, win.at[s_q], slot(w, 0, q, c), dev(w, yy, c))
        frecv(s_hx, k)
        fsend(8, k, win.at[qh_src], qh_dst, qh_to)
        fsend(9, k, win.at[s_q], s_q, mate)
        fsend(10, k, win.at[s_w], s_w, mate)
        fsend(11, k, win.at[s_hx], s_hx, mate)
        relay(12, k, s_lx)
        if k == 0:
            forward_recv_group([flip(own)])
    forward_group([s_q, s_w, s_hx, s_lx])

    for k in range(PARTS_F):
        frecv(s_hw, k)
        fsend(13, k, win.at[s_hw], slot(q, h, w, c), dev(q, yy, c))
        fsend(14, k, win.at[s_hw], s_hw, mate)
        if k == 0:
            forward_recv_group([flip(s_q), flip(s_w)])
    forward_recv_group([flip(s_hx), flip(s_lx)])
    for k in range(PARTS_F):
        relay(15, k, s_o)
        relay(16, k, s_lq)
    forward_group([s_hw, s_o, s_lq])
    for k in range(PARTS_F):
        relay(17, k, s_hq)
    forward_group([s_hq])
    forward_recv_group([flip(s_hw), flip(s_o)])
    relay(18, 0, s_ho)
    forward_recv_group([flip(s_lq)])
    for k in range(1, PARTS_F):
        relay(18, k, s_ho)
    forward_recv_group([flip(s_hq)])
    forward_group([s_ho])
    forward_recv_group([flip(s_ho)])

    k_o = (1 - xl) * 2 + c
    k_m = xl * 2 + 1 - c
    k_mo = (1 - xl) * 2 + 1 - c

    def chunk(k):
        return acc.at[pl.ds(pl.multiple_of(k * ROWS, ROWS), ROWS)]

    def half_of(k, n):
        return acc.at[pl.ds(pl.multiple_of(k * ROWS + n * HALF, HALF), HALF)]

    halves = [pl.ds(n * HALF, HALF) for n in range(2)]
    rs0 = [remote(half_of(k_mo, n), rs_in.at[0, halves[n]], rs_s.at[n], rs_r.at[n], mate) for n in range(2)]
    rs1 = [remote(half_of(k_m, n), rs_in.at[1, halves[n]], rs_s.at[2 + n], rs_r.at[2 + n], mate) for n in range(2)]
    rs2 = [remote(rs_send.at[halves[n]], rs_mid.at[halves[n]], rs_s.at[4 + n], rs_r.at[4 + n], dev(q, yy, c)) for n in range(2)]
    for cp in rs0 + rs1:
        cp.start()
    for cp in sends:
        cp.wait_send()
    for n in range(2):
        rs0[n].wait_recv()
        rs_send[halves[n]] = half_of(k_o, n)[...] + rs_in[0, halves[n]]
        rs2[n].start()
    cot_cp.wait()
    w_cp.wait()
    wh, wl = split(w_v[...])

    def gt_copy(k, n, number, to):
        return remote(gt.at[k, n], gt.at[k, n], ag_s.at[number, n], ag_r.at[k, n], to)

    def grecv(k, n):
        gt_copy(k, n, 0, mate).wait_recv()

    ag = []
    aggs, gps = [], []
    for n in range(2):
        rs1[n].wait_recv()
        part = half_of(rep, n)[...] + rs_in[1, halves[n]]
        rs2[n].wait_recv()
        agg = part + rs_mid[halves[n]]
        ah, al = split(agg)
        pre = dot(ah, wh) + (dot(al, wh) + dot(ah, wl))
        sig = jax.nn.sigmoid(pre)
        gp = cot_v[halves[n]] * (sig * (1.0 + pre * (1.0 - sig)))
        ph, plow = split(gp)
        gt[rep, n] = dot_t(wh, ph) + (dot_t(wl, ph) + dot_t(wh, plow))
        for number, to in ((0, dev(q, yy, c)), (1, mate)):
            cp = gt_copy(rep, n, number, to)
            cp.start()
            ag.append(cp)
        rs_in[0, halves[n]] = pre * sig
        aggs.append(agg)
        gps.append(gp)
    act_cp = pltpu.make_async_copy(rs_in.at[0], act_out, loc_sem.at[8])
    act_cp.start()
    agg = jnp.concatenate(aggs, axis=0)
    gp = jnp.concatenate(gps, axis=0)
    wg = dot3(dot, agg.T, gp).reshape(PLANE, F // PLANE, F)
    wg_loc[...] = wg

    def ar_copy(d, src, dst, ssem, rsem):
        return remote(src, dst, ssem.at[d], rsem.at[d], plane_dev(lax.rem(m_me + d, PLANE)))

    def aa_copy(d):
        return ar_copy(d, wg_loc.at[lax.rem(m_me + d, PLANE)], ar_a.at[m_me], aa_s, aa_r)

    def ab_copy(d):
        return remote(wg_sum, ar_b.at[zi], ab_s.at[d], ab_r.at[d], (lax.rem(row + 8 * d, nz * 8), rep))

    def ac_copy(d):
        return ar_copy(d, wg_all.at[m_me], wg_all.at[m_me], ac_s, ac_r)

    @pl.loop(1, PLANE)
    def _(d):
        aa_copy(d).start()

    ar_a[m_me] = wg_loc[m_me]

    for n in range(2):
        grecv(k_m, n)

    def spread(pair):
        for core in range(2):
            for n in range(2):
                high, low = split(gt[pair * 2 + core, n])
                start = core * ROWS + n * HALF
                gt_h[pair, :, start:start + HALF] = high
                gt_l[pair, :, start:start + HALF] = low

    def backward(s, pair):
        rows = pl.ds(pl.multiple_of(pair * 2 * ROWS, 2 * ROWS), 2 * ROWS)
        a = dense_h[s, rows, :]
        g = gt_h[pair]
        return dot(g, a) + (dot(gt_l[pair], a) + dot(g, dense_l[s, rows, :]))

    spread(xl)

    def first_pass(slots):
        @pl.loop(0, len(slots))
        def _(i):
            s = choose(i, slots)
            win[s] = backward(s, xl)

    early = [s_ho, s_hw, s_o, s_lq, s_hq, s_q]
    early = [v for s in early for v in (flip(s), s)]
    first_pass(early[:4])
    for n in range(2):
        grecv(k_o, n)
        cp = gt_copy(k_o, n, 2, mate)
        cp.start()
        ag.append(cp)
        if n == 0:
            first_pass(early[4:10])
    first_pass(early[10:])
    for n in range(2):
        grecv(k_mo, n)
    spread(1 - xl)

    def mate_copy(s):
        i = lax.div(s, 2)
        return remote(win.at[s], mrecv.at[i], bm_s.at[i], bm_r.at[i], mate)

    def second_pass(s, whole=False):
        @pl.loop(0, 2)
        def _(i):
            at = jnp.where(i == 0, flip(s), s)
            if whole:
                win[at] = backward(at, xl) + backward(at, 1 - xl)
            else:
                win[at] += backward(at, 1 - xl)

            @pl.when(i == 0)
            def _():
                mate_copy(at).start()

    def add_mate(s):
        mate_copy(s).wait_recv()
        win[s] += mrecv[lax.div(s, 2)]

    back = {}

    def bsend(n, k, s, to):
        part = piece(k, PARTS_B)
        cp = remote(win.at[s, part], rbuf.at[n, part], br_s.at[n, k], br_r.at[n, k], to)
        cp.start()
        back[n, k] = cp

    def bsend_all(n, s, to):
        for k in range(PARTS_B):
            bsend(n, k, s, to)

    def badd(n, k, s):
        part = piece(k, PARTS_B)
        back[n, k].wait_recv()
        win[s, part] += rbuf[n, part]

    from_q, from_y = dev(q, yy, c), dev(x, yy + h, c)
    hq_to = (jnp.where(c == 0, from_q[0], from_y[0]), jnp.where(c == 0, from_q[1], from_y[1]))
    second_pass(s_ho)
    second_pass(s_hw)
    add_mate(s_ho)
    bsend_all(0, s_ho, dev(q, yy, c))
    second_pass(s_o)
    add_mate(s_hw)
    second_pass(s_lq)
    add_mate(s_o)
    bsend_all(1, s_o, dev(w, yy, c))
    second_pass(s_hq)
    add_mate(s_lq)
    bsend_all(2, s_lq, dev(x, yy + l, c))
    second_pass(s_q)
    add_mate(s_hq)
    bsend_all(3, s_hq, hq_to)

    def pass_on_hw(k):
        badd(0, k, s_hw)
        bsend(4, k, s_hw, dev(x, yy + h, c))

    pass_on_hw(0)
    second_pass(s_lx, whole=True)
    pass_on_hw(1)
    add_mate(s_q)
    second_pass(s_hx, whole=True)
    for k in range(2, PARTS_B):
        pass_on_hw(k)
    add_mate(s_lx)
    bsend_all(5, s_lx, dev(x, yy + l, c))
    second_pass(s_w, whole=True)
    @pl.loop(1, PLANE)
    def _(d):
        aa_copy(d).wait_recv()

    total = ar_a[0]
    for k in range(1, PLANE):
        total = total + ar_a[k]
    wg_sum[...] = total
    ar_b[zi] = total

    @pl.loop(1, nz)
    def _(d):
        ab_copy(d).start()

    add_mate(s_hx)
    s_3 = jnp.where(c == 0, s_hx, s_q)

    def pass_on_q(k):
        badd(1, k, s_q)
        badd(2, k, s_q)
        badd(3, k, s_3)
        bsend(6, k, s_q, dev(q, yy, c))
        bsend(7, k, s_hx, dev(x, yy + h, c))

    def pass_on_w(k):
        badd(4, k, s_w)
        bsend(8, k, s_w, dev(w, yy, c))

    pass_on_q(0)
    second_pass(own, whole=True)
    add_mate(s_w)
    pass_on_w(0)
    for k in range(1, PARTS_B):
        pass_on_q(k)
        pass_on_w(k)
    add_mate(own)
    @pl.loop(1, nz)
    def _(d):
        ab_copy(d).wait_recv()

    total = ar_b[0]
    for k in range(1, nz):
        total = total + ar_b[k]
    wg_all[m_me] = total

    @pl.loop(1, PLANE)
    def _(d):
        ac_copy(d).start()

    for k in range(PARTS_B):
        for n in (5, 6, 7, 8):
            badd(n, k, own)
    rs_in[1] = win[own].T
    fg_cp = pltpu.make_async_copy(rs_in.at[1], fg_out, loc_sem.at[9])
    fg_cp.start()

    @pl.loop(1, PLANE)
    def _(d):
        ac_copy(d).wait_recv()

    wg_cp = pltpu.make_async_copy(wg_all, wg_out, loc_sem.at[10])
    wg_cp.start()
    for cp in list(back.values()) + rs0 + rs1 + rs2 + ag:
        cp.wait_send()
    for i in range(WIN // 2):
        mate_copy(2 * i + 1 - c).wait_send()

    @pl.loop(1, PLANE)
    def _(d):
        aa_copy(d).wait_send()
        ac_copy(d).wait_send()

    @pl.loop(1, nz)
    def _(d):
        ab_copy(d).wait_send()

    act_cp.wait()
    fg_cp.wait()
    wg_cp.wait()


def shards(features, weight, cotangent, tile_row, tile_col, tile_count, tile_values):
    nz = lax.axis_size("row") // 8
    anywhere = pl.BlockSpec(memory_space=pl.ANY)
    sem = pltpu.SemaphoreType.DMA
    act, fg, wg = pl.pallas_call(
        kernel,
        out_shape=(
            jax.ShapeDtypeStruct((ROWS, F), F32),
            jax.ShapeDtypeStruct((ROWS, F), F32),
            jax.ShapeDtypeStruct((PLANE, F // PLANE, F), F32),
        ),
        in_specs=[anywhere] * 7,
        out_specs=(anywhere,) * 3,
        scratch_shapes=[
            pltpu.VMEM((SLOTS, TILE, TILE), F32),
            pltpu.VMEM((SLOTS + 1, TILE, TILE), F32),
            pltpu.VMEM((WIN, TPB * TILE, 2 * TILE), BF16),
            pltpu.VMEM((WIN, TPB * TILE, 2 * TILE), BF16),
            pltpu.VMEM((WIN, ROWS, F), F32),
            pltpu.VMEM((4 * ROWS, F), F32),
            pltpu.VMEM((2, ROWS, F), F32),
            pltpu.VMEM((ROWS, F), F32),
            pltpu.VMEM((ROWS, F), F32),
            pltpu.VMEM((4, 2, F, HALF), F32),
            pltpu.VMEM((2, F, 2 * ROWS), BF16),
            pltpu.VMEM((2, F, 2 * ROWS), BF16),
            pltpu.VMEM((WIN // 2, F, ROWS), F32),
            pltpu.VMEM((9, F, ROWS), F32),
            pltpu.VMEM((PLANE, F // PLANE, F), F32),
            pltpu.VMEM((PLANE, F // PLANE, F), F32),
            pltpu.VMEM((nz, F // PLANE, F), F32),
            pltpu.VMEM((F // PLANE, F), F32),
            pltpu.VMEM((PLANE, F // PLANE, F), F32),
            pltpu.VMEM((ROWS, F), F32),
            pltpu.VMEM((F, F), F32),
            pltpu.VMEM((1, 1, SLOTS), jnp.int32),
            pltpu.VMEM((1, 1, SLOTS), jnp.int32),
            pltpu.VMEM((1, 1), jnp.int32),
            pltpu.VMEM((8, SLOTS), jnp.int32),
            pltpu.SMEM((8, SLOTS), jnp.int32),
            sem((11,)), sem((19, PARTS_F)), sem((WIN, PARTS_F)), sem((6,)), sem((6,)), sem((3, 2)), sem((4, 2)),
            sem((WIN // 2,)), sem((WIN // 2,)), sem((9, PARTS_B)), sem((9, PARTS_B)),
            sem((PLANE,)), sem((PLANE,)), sem((nz,)), sem((nz,)), sem((PLANE,)), sem((PLANE,)),
        ],
        compiler_params=pltpu.CompilerParams(
            collective_id=0, has_side_effects=True, vmem_limit_bytes=62 * 1024 * 1024
        ),
    )(features, weight, cotangent, tile_values[0, 0], tile_row, tile_col, tile_count)
    shape = jax.ShapeDtypeStruct((ROWS, F), F32)
    return pl.pallas_call(
        deliver,
        out_shape=(shape,) * 3,
        in_specs=[anywhere] * 3,
        out_specs=(anywhere,) * 3,
        scratch_shapes=[pltpu.VMEM((3, ROWS, F), F32), sem((3,)), sem((3,))],
    )(act, fg, wg.reshape(F, F))


def solution(mesh):
    placed = (
        P(("row", "rep"), None),
        P(),
        P(("row", "rep"), None),
        P("row", "rep", None),
        P("row", "rep", None),
        P("row", "rep"),
        P("row", "rep", None, None, None),
    )
    return jax.shard_map(
        shards,
        mesh=mesh,
        in_specs=placed,
        out_specs=(P(("row", "rep"), None), P(("row", "rep"), None), P()),
        check_vma=False,
    )
```

time: 105 us -> 83.1 us (0.79)
  Pallas kernels: 94.5 us -> 81.2 us
  local copies, waits for them, and re-layouts: 5.01 us -> 0 us
  other arithmetic: 3.19 us -> 0 us
    pallas_call x1, Pallas kernels: 94.5 us -> 79.4 us  [shards(): pl.pallas_call(kernel, out_shape=(jax.ShapeDtypeStruct((ROWS, F), F32), j...]
    unnamed x3 -> x0, local copies, waits for them, and re-layouts: 5.01 us -> none
    pallas_call x0 -> x1, Pallas kernels: none -> 1.88 us  [shards(): pl.pallas_call(deliver, out_shape=(shape,) * 3, in_specs=[anywhere] * 3,...]
    reduce_sum x4 -> x0, other arithmetic: 1.59 us -> none  [the longest x1 0.64 us: shards(): keep = jnp.sum(jnp.where(hit & ~first[None, :], 1.0, 0.0), axis=1)]
    select_n x2 -> x0, other arithmetic: 1.27 us -> none  [the longest x1 0.68 us: shards(): key = jnp.where(live, tile_rows * BAND_TILES + position, places + slot_ids)]
where the time goes in v2:
time: 83.1 us; the launch traced here: 82.7 us
  Pallas kernels  81.2 us (98%)
  between operations  1.45 us (2%)
    pallas_call x1, Pallas kernels, shards(): pl.pallas_call(kernel, out_shape=(jax.ShapeDtypeStruct((ROWS, F), F32), j...  79.4 us
    pallas_call x1, Pallas kernels, shards(): pl.pallas_call(deliver, out_shape=(shape,) * 3, in_specs=[anywhere] * 3,...  1.88 us

profile of v2, /device:TPU:1, one launch (start us, length us, event | category | flops | bytes accessed | tf_op | source)
XLA Modules:
  0.0 82.7 jit_solution(6123889067742289279)
XLA Ops:
  1.3 79.4 %shard_map.94 = (f32[256,256]{1,0:T(8,128)}, f32[256,256]{1,0:T(8,128)}, f32[32,8,256]{2,1,0:T(8,128)}) custom-call(f32[256,256]{1,0:T(8,128)} %feat.1, f32[256,256]{1,0:T(8,128)} %weight.1, f32[256,256]{1,0:T(8,128)} %cot.1, f32[128,128,128]{2,1,0:T(8,128)} %bitcast.2, s32[1,1,128]{2,1,0:T(1,128)} %tile_row.1, s32[1,1,128]{2,1,0:T(1,128)} %tile_col.1, ...), custom_call_target="tpu_custom_call" | custom-call | tf_op jit(solution)/shard_map/pallas_call | solution.py:568
  80.7 1.9 %shard_map.95 = (f32[256,256]{1,0:T(8,128)}, f32[256,256]{1,0:T(8,128)}, f32[256,256]{1,0:T(8,128)}) custom-call(f32[256,256]{1,0:T(8,128)} %get-tuple-element.6.act, f32[256,256]{1,0:T(8,128)} %get-tuple-element.7.fg, f32[256,256]{1,0:T(8,128)} %bitcast.3), custom_call_target="tpu_custom_call" | custom-call | tf_op jit(solution)/shard_map/pallas_call | solution.py:613

commit v3 on v2

--- a/solution.py
+++ b/solution.py
@@ -79,19 +79,6 @@
         upto = total(ones(key_c <= spot))
         there = total(ones(key_c == spot))
         plan[2 + part:3 + part, :] = jnp.where(there > 0, upto - 1, SLOTS)
-
-
-def deliver(act, fg, wg, act_out, fg_out, wg_out, stage, sem_in, sem_out):
-    pairs = ((act, act_out), (fg, fg_out), (wg, wg_out))
-    inward = [pltpu.make_async_copy(src, stage.at[i], sem_in.at[i]) for i, (src, _) in enumerate(pairs)]
-    outward = [pltpu.make_async_copy(stage.at[i], dst, sem_out.at[i]) for i, (_, dst) in enumerate(pairs)]
-    for cp in inward:
-        cp.start()
-    for cp, onward in zip(inward, outward):
-        cp.wait()
-        onward.start()
-    for cp in outward:
-        cp.wait()
 
 
 def kernel(
@@ -283,10 +270,9 @@
     forward_group([s_hw, s_o, s_lq])
     for k in range(PARTS_F):
         relay(17, k, s_hq)
+    relay(18, 0, s_ho)
     forward_group([s_hq])
-    forward_recv_group([flip(s_hw), flip(s_o)])
-    relay(18, 0, s_ho)
-    forward_recv_group([flip(s_lq)])
+    forward_recv_group([flip(s_hw), flip(s_o), flip(s_lq)])
     for k in range(1, PARTS_F):
         relay(18, k, s_ho)
     forward_recv_group([flip(s_hq)])
@@ -353,20 +339,16 @@
     wg_loc[...] = wg
 
     def ar_copy(d, src, dst, ssem, rsem):
-        return remote(src, dst, ssem.at[d], rsem.at[d], plane_dev(lax.rem(m_me + d, PLANE)))
+        return remote(src, dst, ssem, rsem, plane_dev(lax.rem(m_me + d, PLANE)))
 
     def aa_copy(d):
         return ar_copy(d, wg_loc.at[lax.rem(m_me + d, PLANE)], ar_a.at[m_me], aa_s, aa_r)
 
     def ab_copy(d):
-        return remote(wg_sum, ar_b.at[zi], ab_s.at[d], ab_r.at[d], (lax.rem(row + 8 * d, nz * 8), rep))
+        return remote(wg_sum, ar_b.at[zi], ab_s, ab_r, (lax.rem(row + 8 * d, nz * 8), rep))
 
     def ac_copy(d):
         return ar_copy(d, wg_all.at[m_me], wg_all.at[m_me], ac_s, ac_r)
-
-    @pl.loop(1, PLANE)
-    def _(d):
-        aa_copy(d).start()
 
     ar_a[m_me] = wg_loc[m_me]
 
@@ -405,6 +387,22 @@
         ag.append(cp)
         if n == 0:
             first_pass(early[4:10])
+    def aa_all():
+        some = pl.ds(0, PLANE - 1)
+        return remote(wg_loc.at[some], ar_a.at[some], aa_s, aa_r, mate)
+
+    def ab_all():
+        some = pl.ds(0, nz - 1)
+        return remote(ar_b.at[some], ar_b.at[some], ab_s, ab_r, mate)
+
+    def ac_all():
+        some = pl.ds(0, PLANE - 1)
+        return remote(wg_all.at[some], wg_all.at[some], ac_s, ac_r, mate)
+
+    @pl.loop(1, PLANE)
+    def _(d):
+        aa_copy(d).start()
+
     first_pass(early[10:])
     for n in range(2):
         grecv(k_mo, n)
@@ -465,6 +463,18 @@
     second_pass(s_q)
     add_mate(s_hq)
     bsend_all(3, s_hq, hq_to)
+    aa_all().wait_recv()
+
+    total = ar_a[0]
+    for k in range(1, PLANE):
+        total = total + ar_a[k]
+    wg_sum[...] = total
+    ar_b[zi] = total
+
+    @pl.loop(1, nz)
+    def _(d):
+        ab_copy(d).start()
+
 
     def pass_on_hw(k):
         badd(0, k, s_hw)
@@ -480,19 +490,16 @@
     add_mate(s_lx)
     bsend_all(5, s_lx, dev(x, yy + l, c))
     second_pass(s_w, whole=True)
+    ab_all().wait_recv()
+
+    total = ar_b[0]
+    for k in range(1, nz):
+        total = total + ar_b[k]
+    wg_all[m_me] = total
+
     @pl.loop(1, PLANE)
     def _(d):
-        aa_copy(d).wait_recv()
-
-    total = ar_a[0]
-    for k in range(1, PLANE):
-        total = total + ar_a[k]
-    wg_sum[...] = total
-    ar_b[zi] = total
-
-    @pl.loop(1, nz)
-    def _(d):
-        ab_copy(d).start()
+        ac_copy(d).start()
 
     add_mate(s_hx)
     s_3 = jnp.where(c == 0, s_hx, s_q)
@@ -516,45 +523,42 @@
         pass_on_q(k)
         pass_on_w(k)
     add_mate(own)
-    @pl.loop(1, nz)
-    def _(d):
-        ab_copy(d).wait_recv()
-
-    total = ar_b[0]
-    for k in range(1, nz):
-        total = total + ar_b[k]
-    wg_all[m_me] = total
-
-    @pl.loop(1, PLANE)
-    def _(d):
-        ac_copy(d).start()
-
     for k in range(PARTS_B):
-        for n in (5, 6, 7, 8):
-            badd(n, k, own)
+        badd(5, k, own)
+
+    ac_all().wait_recv()
+
+    wg_cp = pltpu.make_async_copy(wg_all, wg_out, loc_sem.at[10])
+    wg_cp.start()
+    for cp in rs0 + rs1 + rs2 + ag:
+        cp.wait_send()
+    for i in range(WIN // 2):
+        mate_copy(2 * i + 1 - c).wait_send()
+
+    aa_all().wait_send()
+
+    ab_all().wait_send()
+
+    for n in range(6):
+        for k in range(PARTS_B):
+            back[n, k].wait_send()
+    for k in range(PARTS_B):
+        badd(6, k, own)
+        badd(7, k, own)
+
+    ac_all().wait_send()
+
+    for n in (6, 7):
+        for k in range(PARTS_B):
+            back[n, k].wait_send()
+    for k in range(PARTS_B):
+        badd(8, k, own)
     rs_in[1] = win[own].T
     fg_cp = pltpu.make_async_copy(rs_in.at[1], fg_out, loc_sem.at[9])
     fg_cp.start()
 
-    @pl.loop(1, PLANE)
-    def _(d):
-        ac_copy(d).wait_recv()
-
-    wg_cp = pltpu.make_async_copy(wg_all, wg_out, loc_sem.at[10])
-    wg_cp.start()
-    for cp in list(back.values()) + rs0 + rs1 + rs2 + ag:
-        cp.wait_send()
-    for i in range(WIN // 2):
-        mate_copy(2 * i + 1 - c).wait_send()
-
-    @pl.loop(1, PLANE)
-    def _(d):
-        aa_copy(d).wait_send()
-        ac_copy(d).wait_send()
-
-    @pl.loop(1, nz)
-    def _(d):
-        ab_copy(d).wait_send()
+    for k in range(PARTS_B):
+        back[8, k].wait_send()
 
     act_cp.wait()
     fg_cp.wait()
@@ -568,9 +572,9 @@
     act, fg, wg = pl.pallas_call(
         kernel,
         out_shape=(
-            jax.ShapeDtypeStruct((ROWS, F), F32),
-            jax.ShapeDtypeStruct((ROWS, F), F32),
-            jax.ShapeDtypeStruct((PLANE, F // PLANE, F), F32),
+            pltpu.VMEM((ROWS, F), F32),
+            pltpu.VMEM((ROWS, F), F32),
+            pltpu.VMEM((PLANE, F // PLANE, F), F32),
         ),
         in_specs=[anywhere] * 7,
         out_specs=(anywhere,) * 3,
@@ -603,20 +607,13 @@
             pltpu.SMEM((8, SLOTS), jnp.int32),
             sem((11,)), sem((19, PARTS_F)), sem((WIN, PARTS_F)), sem((6,)), sem((6,)), sem((3, 2)), sem((4, 2)),
             sem((WIN // 2,)), sem((WIN // 2,)), sem((9, PARTS_B)), sem((9, PARTS_B)),
-            sem((PLANE,)), sem((PLANE,)), sem((nz,)), sem((nz,)), sem((PLANE,)), sem((PLANE,)),
+            *[sem] * 6,
         ],
         compiler_params=pltpu.CompilerParams(
             collective_id=0, has_side_effects=True, vmem_limit_bytes=62 * 1024 * 1024
         ),
     )(features, weight, cotangent, tile_values[0, 0], tile_row, tile_col, tile_count)
-    shape = jax.ShapeDtypeStruct((ROWS, F), F32)
-    return pl.pallas_call(
-        deliver,
-        out_shape=(shape,) * 3,
-        in_specs=[anywhere] * 3,
-        out_specs=(anywhere,) * 3,
-        scratch_shapes=[pltpu.VMEM((3, ROWS, F), F32), sem((3,)), sem((3,))],
-    )(act, fg, wg.reshape(F, F))
+    return act, fg, wg.reshape(F, F)
 
 
 def solution(mesh):

time: 83.1 us -> 81.4 us (0.980)
  Pallas kernels: 81.2 us -> 77.9 us
  local copies, waits for them, and re-layouts: 0 us -> 2.11 us
    pallas_call x2 -> x1, Pallas kernels: 81.2 us -> 77.9 us  [shards(): pl.pallas_call(kernel, out_shape=(pltpu.VMEM((ROWS, F), F32), pltpu.VMEM(...]
    unnamed x0 -> x3, local copies, waits for them, and re-layouts: none -> 2.11 us
where the time goes in v3:
time: 81.4 us; the launch traced here: 81.3 us
  Pallas kernels  77.9 us (96%)
  local copies, waits for them, and re-layouts  2.11 us (3%)
  between operations  1.29 us (2%)
    pallas_call x1, Pallas kernels, shards(): pl.pallas_call(kernel, out_shape=(pltpu.VMEM((ROWS, F), F32), pltpu.VMEM(...  77.9 us
    unnamed x3, local copies, waits for them, and re-layouts  2.11 us

profile of v3, /device:TPU:1, one launch (start us, length us, event | category | flops | bytes accessed | tf_op | source)
XLA Modules:
  0.0 81.3 jit_solution(730518706044496711)
XLA Ops:
  1.3 77.9 %shard_map.94 = (f32[256,256]{1,0:T(8,128)S(1)}, f32[256,256]{1,0:T(8,128)S(1)}, f32[32,8,256]{2,1,0:T(8,128)S(1)}) custom-call(f32[256,256]{1,0:T(8,128)} %feat.1, f32[256,256]{1,0:T(8,128)} %weight.1, f32[256,256]{1,0:T(8,128)} %cot.1, f32[128,128,128]{2,1,0:T(8,128)} %bitcast.3, s32[1,1,128]{2,1,0:T(1,128)} %tile_row.1, s32[1,1,128]{2,1,0:T(1,128)} %tile_col.1, ...), custom_call_target="tpu_custom_call" | custom-call | tf_op jit(solution)/shard_map/pallas_call | solution.py:572
  79.2 0.7 copy.13
  79.9 0.7 copy.14
  80.6 0.7 copy.15

commit v4 on v3

--- a/solution.py
+++ b/solution.py
@@ -328,11 +328,9 @@
             cp = gt_copy(rep, n, number, to)
             cp.start()
             ag.append(cp)
-        rs_in[0, halves[n]] = pre * sig
+        act_out[halves[n]] = pre * sig
         aggs.append(agg)
         gps.append(gp)
-    act_cp = pltpu.make_async_copy(rs_in.at[0], act_out, loc_sem.at[8])
-    act_cp.start()
     agg = jnp.concatenate(aggs, axis=0)
     gp = jnp.concatenate(gps, axis=0)
     wg = dot3(dot, agg.T, gp).reshape(PLANE, F // PLANE, F)
@@ -528,8 +526,7 @@
 
     ac_all().wait_recv()
 
-    wg_cp = pltpu.make_async_copy(wg_all, wg_out, loc_sem.at[10])
-    wg_cp.start()
+    wg_out[...] = wg_all[...]
     for cp in rs0 + rs1 + rs2 + ag:
         cp.wait_send()
     for i in range(WIN // 2):
@@ -553,16 +550,10 @@
             back[n, k].wait_send()
     for k in range(PARTS_B):
         badd(8, k, own)
-    rs_in[1] = win[own].T
-    fg_cp = pltpu.make_async_copy(rs_in.at[1], fg_out, loc_sem.at[9])
-    fg_cp.start()
+    fg_out[...] = win[own].T
 
     for k in range(PARTS_B):
         back[8, k].wait_send()
-
-    act_cp.wait()
-    fg_cp.wait()
-    wg_cp.wait()
 
 
 def shards(features, weight, cotangent, tile_row, tile_col, tile_count, tile_values):
@@ -577,7 +568,7 @@
             pltpu.VMEM((PLANE, F // PLANE, F), F32),
         ),
         in_specs=[anywhere] * 7,
-        out_specs=(anywhere,) * 3,
+        out_specs=(pl.BlockSpec(memory_space=pltpu.VMEM),) * 3,
         scratch_shapes=[
             pltpu.VMEM((SLOTS, TILE, TILE), F32),
             pltpu.VMEM((SLOTS + 1, TILE, TILE), F32),
@@ -605,7 +596,7 @@
             pltpu.VMEM((1, 1), jnp.int32),
             pltpu.VMEM((8, SLOTS), jnp.int32),
             pltpu.SMEM((8, SLOTS), jnp.int32),
-            sem((11,)), sem((19, PARTS_F)), sem((WIN, PARTS_F)), sem((6,)), sem((6,)), sem((3, 2)), sem((4, 2)),
+            sem((8,)), sem((19, PARTS_F)), sem((WIN, PARTS_F)), sem((6,)), sem((6,)), sem((3, 2)), sem((4, 2)),
             sem((WIN // 2,)), sem((WIN // 2,)), sem((9, PARTS_B)), sem((9, PARTS_B)),
             *[sem] * 6,
         ],

time: 81.4 us -> 81.4 us (level)
  no operation moved by 1% of the time
where the time goes in v4:
time: 81.4 us; the launch traced here: 81.3 us
  Pallas kernels  77.9 us (96%)
  local copies, waits for them, and re-layouts  2.11 us (3%)
  between operations  1.29 us (2%)
    pallas_call x1, Pallas kernels, shards(): pl.pallas_call(kernel, out_shape=(pltpu.VMEM((ROWS, F), F32), pltpu.VMEM(...  77.9 us
    unnamed x3, local copies, waits for them, and re-layouts  2.11 us

profile of v4, /device:TPU:1, one launch (start us, length us, event | category | flops | bytes accessed | tf_op | source)
XLA Modules:
  0.0 81.3 jit_solution(3095009556477950689)
XLA Ops:
  1.3 77.9 %shard_map.94 = (f32[256,256]{1,0:T(8,128)S(1)}, f32[256,256]{1,0:T(8,128)S(1)}, f32[32,8,256]{2,1,0:T(8,128)S(1)}) custom-call(f32[256,256]{1,0:T(8,128)} %feat.1, f32[256,256]{1,0:T(8,128)} %weight.1, f32[256,256]{1,0:T(8,128)} %cot.1, f32[128,128,128]{2,1,0:T(8,128)} %bitcast.3, s32[1,1,128]{2,1,0:T(1,128)} %tile_row.1, s32[1,1,128]{2,1,0:T(1,128)} %tile_col.1, ...), custom_call_target="tpu_custom_call" | custom-call | tf_op jit(solution)/shard_map/pallas_call | solution.py:563
  79.2 0.7 copy.13
  79.9 0.7 copy.14
  80.6 0.7 copy.15
